TPU v7x, 128 devices: a whole 4x4x4 slice. The times are simulated.
128 devices in a mesh: intra: 16 (over z, x), cross: 8 (over y, core).
Axes of the slice: x: 4, y: 4, z: 4, core: 2. Of those that a mesh axis runs over, the one named last changes fastest.
Arguments:
- tokens: bfloat16 [131072, 4096], P(('intra', 'cross')), may hold values from -80 to 80
- norm_gain: bfloat16 [4096], P(('intra', 'cross')), may hold values from 0.5 to 1.5
- weight_codes: bfloat16 [4096, 1024], P(('intra', 'cross')), may hold values from -127 to 127, as said below
- block_scales: bfloat16 [2048], P(('intra', 'cross')), may hold values from 9.9658966e-05 to 0.00039863586
- upstream: bfloat16 [131072, 1024], P(('intra', 'cross')), may hold values from -6 to 6
- loss_mask: int32 [131072], P(('intra', 'cross')), may hold values 0 or 1
Outputs:
- projected: bfloat16 [131072, 1024], P(('intra', 'cross'))
- grad_tokens: bfloat16 [131072, 4096], P(('intra', 'cross'))
- grad_weight: float32 [4096, 1024], P(('intra', 'cross'))
- grad_gain: float32 [4096], P(('intra', 'cross'))
Inputs may be any that keep to these rules, and one draw needn't show every extreme that they name: `weight_codes`: integer values.
All inputs are finite; a program needn't handle non-finite values. No bound on the sum of `loss_mask` on one device may be relied on, other than what follows from the above.
Results may differ from a plain program's by a relative error of at most 0.0058.
Values may be sent and summed in bfloat16 or wider, within the bound.
A program may use at most 192 MiB of HBM per device.

v0:
```python
import jax
import jax.numpy as jnp
from jax import lax
from jax.sharding import PartitionSpec as P


def dequantize(piece_codes, piece_scales):
    return (piece_codes.astype(jnp.float32) * piece_scales.astype(jnp.float32)[:, None]).astype(
        jnp.bfloat16
    )


def shards(tokens, norm_gain, weight_codes, block_scales, upstream, loss_mask):
    values = tokens.astype(jnp.float32)
    inverse = lax.rsqrt(jnp.mean(values * values, axis=1, keepdims=True) + 1e-05)
    unit_rows = values * inverse
    repeat_count = weight_codes.shape[0] // block_scales.shape[0]
    row_scales = jnp.repeat(block_scales, repeat_count)
    masked = upstream * loss_mask.astype(jnp.bfloat16)[:, None]
    piece_codes = lax.all_gather(weight_codes, ("intra", "cross"), axis=0, tiled=True)
    piece_gain = lax.all_gather(norm_gain, ("intra", "cross"), axis=0, tiled=True)
    piece_scales = lax.all_gather(row_scales, ("intra", "cross"), axis=0, tiled=True)
    normed_piece = (unit_rows * piece_gain.astype(jnp.float32)[None, :]).astype(jnp.bfloat16)
    summed = jnp.dot(
        normed_piece, dequantize(piece_codes, piece_scales), preferred_element_type=jnp.float32
    )
    normed = normed_piece
    gathered_gain = piece_gain
    summed, normed, gathered_gain = (summed, normed, gathered_gain)
    pieces = lax.all_gather((weight_codes, row_scales), ("intra", "cross"), axis=0, tiled=True)
    weight_rows = dequantize(pieces[0], pieces[1])
    grad_normed = lax.dot_general(
        masked, weight_rows, (((1,), (1,)), ((), ())), preferred_element_type=jnp.float32
    )
    projected = summed.astype(jnp.bfloat16)
    grad_scaled = grad_normed * gathered_gain.astype(jnp.float32)[None, :]
    grad_tokens = (
        inverse
        * (grad_scaled - unit_rows * jnp.mean(grad_scaled * unit_rows, axis=1, keepdims=True))
    ).astype(jnp.bfloat16)
    part_weight = lax.dot_general(
        normed, masked, (((0,), (0,)), ((), ())), preferred_element_type=jnp.float32
    )
    part_gain = jnp.sum(grad_normed * unit_rows, axis=0)
    grad_weight, grad_gain = (
        lax.psum_scatter(part_weight, ("intra", "cross"), scatter_dimension=0, tiled=True),
        lax.psum_scatter(part_gain, ("intra", "cross"), scatter_dimension=0, tiled=True),
    )
    return (projected, grad_tokens, grad_weight, grad_gain)


def solution(mesh):
    return jax.shard_map(
        shards,
        mesh=mesh,
        in_specs=(
            P(("intra", "cross"), None),
            P(("intra", "cross")),
            P(("intra", "cross"), None),
            P(("intra", "cross")),
            P(("intra", "cross"), None),
            P(("intra", "cross")),
        ),
        out_specs=(
            P(("intra", "cross"), None),
            P(("intra", "cross"), None),
            P(("intra", "cross"), None),
            P(("intra", "cross")),
        ),
        check_vma=False,
    )
```

profile of v0, /device:TPU:1, one launch (start us, length us, event | category | flops | bytes accessed | tf_op | source)
XLA Modules:
  0.0 763.8 jit_solution(3089815878551138269)
XLA Ops:
  7.2 0.0 all-gather.2.cloned.1.call-start
  7.2 0.7 all-gather.2.cloned.1.call-update
  7.9 0.0 reduce-scatter.2.cloned.1.call-start
  8.0 0.7 convert_element_type.38
  8.6 0.7 broadcast_in_dim.2
  9.4 0.1 reshape.29
  9.5 0.2 dynamic-update-slice.1
  9.7 0.8 dynamic-update-slice
  10.6 69.7 %all-reduce.3 = (bf16[4096]{0:T(1024)(128)(2,1)S(1)}, bf16[4096]{0:T(1024)(128)(2,1)S(1)}) all-reduce(bf16[4096]{0:T(1024)(128)(2,1)S(1)} %dynamic-update-slice.1, bf16[4096]{0:T(1024)(128)(2,1)S(1)} %dynamic-update-slice), channel_id=1, replica_groups=mesh['intra'=16,'cross'=8] {'intra','cross'}, use_global_device_ids=true, to_apply=%add.1 | all-reduce | flops 8192 | bytes 32768
  80.3 5.2 fusion.10
  85.5 15.8 %fusion.13 = f32[4096,1024]{1,0:T(8,128)} fusion(bf16[1024,4096]{1,0:T(8,128)(2,1)} %param.6, f32[4096]{0:T(1024)S(1)} %convert_element_type.32, f32[1024]{0:T(1024)S(1)} %add_rsqrt_fusion, bf16[1024,1024]{1,0:T(8,128)(2,1)} %param.10, bf16[1024]{0:T(1024)(128)(2,1)S(1)} %convert_element_type.38), kind=kOutput, calls=%fused_computation.16 | convolution fusion | flops 8607760384 | bytes 27285504 | tf_op jit(solution)/shard_map/dot_general | solution.py:41
  101.4 0.0 copy-start.1
  101.4 0.0 reduce-scatter.2.cloned.1.call-update
  101.4 0.0 all-gather.2.cloned.1.call-done
  101.4 1.5 copy-done.1
  103.0 16.6 %fusion.9 = (f32[4096]{0:T(1024)S(1)}, f32[1024]{0:T(1024)S(1)}, f32[1024,4096]{1,0:T(8,128)}) fusion(bf16[1024,4096]{1,0:T(8,128)(2,1)} %param.6, f32[1024]{0:T(1024)S(1)} %add_rsqrt_fusion, f32[4096]{0:T(1024)S(1)} %convert_element_type.32, bf16[4096,1024]{1,0:T(8,128)(2,1)} %all-gather.2.cloned.1.call-done, f32[4096]{0:T(1024)S(1)} %convert_element_type.35, ...), kind=kOutput, calls=%fused_computation.11 | convolution fusion | flops 8632921088 | bytes 35710976 | tf_op jit(solution)/shard_map/dot_general | solution.py:32
  119.5 63.8 %all-reduce.2 = f32[4096]{0:T(1024)S(1)} all-reduce(f32[4096]{0:T(1024)S(1)} %get-tuple-element.4), channel_id=3, replica_groups=mesh['intra'=16,'cross'=8] {'intra','cross'}, use_global_device_ids=true, to_apply=%region_4.0.clone | all-reduce | flops 4096 | bytes 32768
  183.4 0.6 dynamic-slice
  184.0 0.0 copy-start
  184.0 13.0 %fusion.8 = bf16[1024,4096]{1,0:T(8,128)(2,1)} fusion(bf16[1024,4096]{1,0:T(8,128)(2,1)} %param.6, f32[1024,4096]{1,0:T(8,128)} %get-tuple-element.8, f32[1024]{0:T(1024)S(1)} %broadcast_multiply_fusion, f32[4096]{0:T(1024)S(1)} %convert_element_type.32, f32[1024]{0:T(1024)S(1)} %add_rsqrt_fusion), kind=kLoop, calls=%fused_computation.10 | loop fusion | flops 29360128 | bytes 33579008 | tf_op jit(solution)/shard_map/convert_element_type | solution.py:40
  197.0 0.4 copy-done
  197.4 12.7 %fusion.16 = bf16[1024,1024]{1,0:T(8,128)(2,1)} fusion(bf16[4096,1024]{1,0:T(8,128)(2,1)S(1)} %copy-done, f32[4096]{0:T(1024)S(1)} %convert_element_type.35, bf16[1024,4096]{1,0:T(8,128)(2,1)} %param.6, f32[4096]{0:T(1024)S(1)} %convert_element_type.32, f32[1024]{0:T(1024)S(1)} %add_rsqrt_fusion), kind=kOutput, calls=%fused_computation.17 | convolution fusion | flops 8620343296 | bytes 18911232 | tf_op jit(solution)/shard_map/dot_general | solution.py:24
  210.1 546.8 %reduce-scatter.2.cloned.1.call-done = f32[32,1024]{1,0:T(8,128)} async-done(((f32[4096,1024]{1,0:T(8,128)}), f32[32,1024]{1,0:T(8,128)}) %reduce-scatter.2.cloned.1.call-update) | async-done | bytes 131088 | tf_op jit(solution)/shard_map/reduce_scatter | solution.py:46
  (6 shorter events, 0.0 us)
Async XLA Ops:
  7.2 94.3 %all-gather.2.cloned.1.call-start = ((), (), s32[]{:S(2)}) async-start(), calls=%async_computation.1 | async-start | bytes 8454144 | tf_op jit(solution)/shard_map/all_gather | solution.py:20
  7.9 749.0 %reduce-scatter.2.cloned.1.call-start = ((), (), s32[]{:S(2)}) async-start(), calls=%async_computation.2 | async-start | bytes 16908288 | tf_op jit(solution)/shard_map/reduce_scatter | solution.py:46
  101.4 1.6 copy-start.1
  184.0 13.5 %copy-start = (bf16[4096,1024]{1,0:T(8,128)(2,1)S(1)}, bf16[4096,1024]{1,0:T(8,128)(2,1)}, u32[]{:S(2)}) copy-start(bf16[4096,1024]{1,0:T(8,128)(2,1)} %all-gather.2.cloned.1.call-done) | copy-start | bytes 25165828
Sparse Core Ops, SparseCore 0:
  11.0 74.1 all-gather.1
  101.5 655.3 reduce-scatter.1
where the time goes:
time: 771 us; the launch traced here: 764 us
  waiting for transfers between devices  548 us (71%)
  blocking collectives  134 us (17%)
  matrix products  45.1 us (6%)
  other arithmetic  18.9 us (2%)
  between operations  14.1 us (2%)
    reduce_scatter x1, waiting for transfers between devices, shards(): lax.psum_scatter(part_weight, ('intra', 'cross'), scatter_dimension=0, ti...  547 us
    unnamed x2, blocking collectives  134 us
    dot_general x1, matrix products, shards(): lax.dot_general(masked, weight_rows, (((1,), (1,)), ((), ())), preferred_...  16.6 us
    dot_general x1, matrix products, shards(): lax.dot_general(normed, masked, (((0,), (0,)), ((), ())), preferred_eleme...  15.8 us
  transfers between devices with their start and end apart: 2, of which 1 were waited for; matrix products, arithmetic and copies ran while one was open for 9% of the time, Pallas kernels for 0%

commit v1 on v0

v1 whole, which is shorter than its diff:
```python
import jax
import jax.numpy as jnp
from jax import lax
from jax.experimental import pallas as pl
from jax.experimental.pallas import tpu as pltpu
from jax.sharding import PartitionSpec as P

MESH = pl.DeviceIdType.MESH
F32 = jnp.float32
BF16 = jnp.bfloat16
D = 4096
KV = 1024
TOK = 1024
ROWS = 32
TILE = 256
COLS = (384, 384, 256)
ORDERS = ((0, 1, 2), (1, 2, 0), (2, 0, 1))
PARTS = range(3)
STEPS = (1, -1, 2)
CHUNKS = (0, 1, -1, 2)
PLANES = (0, -1, 1, 2)


def piece(part, stage, pos, at, half=None):
    order = ORDERS[part]
    index = [None, None, None, pos[3], slice(None), slice(None)]
    for axis in order[:stage]:
        index[axis] = pos[axis]
    index[order[stage]] = at
    free = order[stage + 1 :]
    for axis in free:
        index[axis] = slice(None)
    if half is not None:
        if free:
            index[min(free)] = slice(2 * half, 2 * half + 2)
        else:
            index[4] = slice(16 * half, 16 * half + 16)
    return tuple(index)


def kernel(
    tokens, upstream, mask, codes, scales, gain,
    proj, tok, grad_weight, grad_gain,
    up, masked, mi, inv, coef, acc, mine,
    w0, w1, w2, g0, g1, g2, c0, c1, c2,
    r00, r10, r20, r01, r11, r21, r02, r12, r22,
    load_sem, ag_send, ag_recv, fwd_send, fwd_recv, pair_send, pair_recv, rs_send, rs_recv,
):
    gathered = (w0, w1, w2)
    sums = (g0, g1, g2)
    pair = (c0, c1, c2)
    landing = ((r00, r01, r02), (r10, r11, r12), (r20, r21, r22))
    intra, cross = lax.axis_index("intra"), lax.axis_index("cross")
    z, x, y, core = intra // 4, intra % 4, cross // 2, cross % 2
    pos = (z, x, y, core)

    def device(at):
        return (at[0] * 4 + at[1], at[2] * 2 + at[3])

    def shifted(axis, step):
        return (pos[axis] + step + 4) % 4

    def beside(axis, step):
        return device(pos[:axis] + (shifted(axis, step),) + pos[axis + 1 :])

    sibling = device((z, x, y, 1 - core))
    blocks = [shifted(0, step) for step in (2, 1, 3, 0)]

    def remote(src, dst, send, recv, to):
        return pltpu.make_async_remote_copy(
            src_ref=src, dst_ref=dst, send_sem=send, recv_sem=recv, device_id=to, device_id_type=MESH
        )

    def ag_copy(part, stage, slot, arriving):
        axis = ORDERS[part][2 - stage]
        at = shifted(axis, -STEPS[slot]) if arriving else pos[axis]
        ref = gathered[part].at[piece(part, 2 - stage, pos, at)]
        number = part * 22 + stage * 3 + slot
        return remote(ref, ref, ag_send.at[number], ag_recv.at[number], beside(axis, STEPS[slot]))

    def ag_chunk(part, chunk, slot, arriving):
        far, near, last = ORDERS[part]
        side = (1, -1, 1, -1)[slot]
        hops = 1 if slot < 2 else 2
        came = hops if arriving else hops - 1
        index = [None, None, None, core, slice(None), slice(None)]
        index[far] = shifted(far, -side * came)
        index[near] = shifted(near, -CHUNKS[chunk])
        index[last] = slice(None) if slot < 2 else slice(2 * (slot - 2), 2 * (slot - 2) + 2)
        ref = gathered[part].at[tuple(index)]
        number = part * 22 + 6 + chunk * 4 + slot
        return remote(ref, ref, ag_send.at[number], ag_recv.at[number], beside(far, side))

    def forward(part, chunk, slot, arriving):
        far, near, _ = ORDERS[part]
        index = [slice(None), slice(None), slice(None), (1 - core) if arriving else core, slice(None), slice(None)]
        index[far] = shifted(far, PLANES[slot])
        if slot:
            index[near] = shifted(near, -CHUNKS[chunk])
        ref = gathered[part].at[tuple(index)]
        number = part * 13 + (slot and 3 * chunk + slot)
        return remote(ref, ref, fwd_send.at[number], fwd_recv.at[number], sibling)

    def ag_send_out(stage):
        for part in PARTS:
            for slot in range(3):
                ag_copy(part, stage, slot, False).start()

    def ag_wait(stage, slots=range(3)):
        for part in PARTS:
            for slot in slots:
                ag_copy(part, stage, slot, True).wait_recv()

    def chunk_out(chunk):
        for part in PARTS:
            ag_chunk(part, chunk, 0, False).start()
            ag_chunk(part, chunk, 1, False).start()

    def chunk_pass(chunk):
        for part in PARTS:
            for side in (0, 1):
                ag_chunk(part, chunk, side, True).wait_recv()
                ag_chunk(part, chunk, 2 + side, False).start()
                forward(part, chunk, 1 + side, False).start()

    def chunk_end(chunk):
        for part in PARTS:
            ag_chunk(part, chunk, 2, True).wait_recv()
            ag_chunk(part, chunk, 3, True).wait_recv()
            forward(part, chunk, 3, False).start()

    def forward_wait(slot):
        for part in PARTS:
            for chunk in range(4 if slot else 1):
                forward(part, chunk, slot, True).wait_recv()

    def pair_copy(part, i):
        at, k = blocks[i], part * 4 + i
        index = (at, slice(None), slice(None), 1 - core)
        return remote(sums[part].at[index], pair[part].at[at], pair_send.at[k], pair_recv.at[k], sibling)

    def pair_out(i):
        for part in PARTS:
            pair_copy(part, i).start()

    def pair_add(i):
        at = blocks[i]
        for part in PARTS:
            pair_copy(part, i).wait_recv()

            def add(xi, carry, part=part):
                own = sums[part][at, xi, :, core].astype(F32)
                sums[part][at, xi, :, core] = (own + pair[part][at, xi].astype(F32)).astype(BF16)
                return carry

            lax.fori_loop(0, 4, add, 0)

    def rs_remote(part, stage, slot, index, axis, step):
        number = part * 18 + (0, 12, 15)[stage] + slot
        return remote(
            sums[part].at[index], landing[part][stage].at[slot],
            rs_send.at[number], rs_recv.at[number], beside(axis, step),
        )

    def z_copy(slot):
        step, half, side = ((2, 0, 1), (2, 1, -1), (1, 0, 1), (1, 1, 1), (-1, 0, -1), (-1, 1, -1))[slot]
        return rs_remote(0, 0, slot, piece(0, 0, pos, shifted(0, step), half), 0, side)

    def block_index(part, i, at):
        index = [blocks[i], slice(None), slice(None), core, slice(None), slice(None)]
        index[ORDERS[part][0]] = at
        return tuple(index)

    def block_copy(part, i, kind):
        axis = ORDERS[part][0]
        side = ((1 if i < 2 else -1), 1, -1)[kind]
        step = (2, 1, -1)[kind]
        return rs_remote(part, 0, kind * 4 + i, block_index(part, i, shifted(axis, step)), axis, side)

    def rs_begin(i):
        for slot in ((0, 1), (3,), (4,), ())[i]:
            z_copy(slot).start()
        for part in (1, 2):
            block_copy(part, i, 0).start()
            block_copy(part, i, 2 if i < 2 else 1).start()

    def rs_pass_z(slot):
        out = (2, 5)[slot]
        z_copy(slot).wait_recv()
        index = piece(0, 0, pos, shifted(0, (1, -1)[slot]), slot)
        sums[0][index] = (sums[0][index].astype(F32) + landing[0][0][slot].astype(F32)).astype(BF16)
        z_copy(out).start()

    def rs_pass(i):
        for part in (1, 2):
            block_copy(part, i, 0).wait_recv()
            step, kind = (1, 1) if i < 2 else (-1, 2)
            index = block_index(part, i, shifted(ORDERS[part][0], step))
            sums[part][index] = (sums[part][index].astype(F32) + landing[part][0][i].astype(F32)).astype(BF16)
            block_copy(part, i, kind).start()

    def rs_own_z():
        for slot in (2, 3, 4, 5):
            z_copy(slot).wait_recv()
        for half in (0, 1):
            index = piece(0, 0, pos, z, half)
            sums[0][index] = (
                sums[0][index].astype(F32)
                + landing[0][0][2 + half].astype(F32)
                + landing[0][0][4 + half].astype(F32)
            ).astype(BF16)

    def rs_own(part):
        for i in range(4):
            block_copy(part, i, 1).wait_recv()
            block_copy(part, i, 2).wait_recv()
            index = block_index(part, i, pos[ORDERS[part][0]])
            sums[part][index] = (
                sums[part][index].astype(F32)
                + landing[part][0][4 + i].astype(F32)
                + landing[part][0][8 + i].astype(F32)
            ).astype(BF16)

    def rs_copy(part, stage, slot):
        axis = ORDERS[part][stage]
        index = piece(part, stage, pos, shifted(axis, STEPS[slot]))
        return rs_remote(part, stage, slot, index, axis, STEPS[slot])

    def rs_send_out(part, stage):
        for slot in (2, 0, 1):
            rs_copy(part, stage, slot).start()

    def rs_total(part, stage):
        index = piece(part, stage, pos, pos[ORDERS[part][stage]])
        total = sums[part][index].astype(F32)
        for slot in range(3):
            rs_copy(part, stage, slot).wait_recv()
            total = total + landing[part][stage][slot].astype(F32)
        if stage == 1:
            sums[part][index] = total.astype(BF16)
        return total

    def load(i):
        rows = pl.ds(i * TILE, TILE)
        return (
            pltpu.make_async_copy(tokens.at[rows], tok.at[rows], load_sem.at[i]),
            pltpu.make_async_copy(upstream.at[rows], up.at[rows], load_sem.at[4 + i]),
        )

    def norms(i):
        for copy in load(i):
            copy.wait()

        def some(j, carry):
            rows = pl.ds(pl.multiple_of(i * TILE + j * 64, 64), 64)
            values = tok[rows, :].astype(F32)
            inverse = lax.rsqrt(jnp.sum(values * values, axis=1, keepdims=True) * (1.0 / D) + 1e-05)
            inv[rows, :] = inverse
            kept = up[rows, :].astype(F32) * coef[rows, :]
            masked[rows, :] = kept.astype(BF16)
            mi[rows, :] = (kept * inverse).astype(BF16)
            return carry

        lax.fori_loop(0, TILE // 64, some, 0)

    def partial_sums(i):
        zi = blocks[i]
        columns = pl.ds(pl.multiple_of(zi * 1024, 1024), 1024)
        part_sum = lax.dot_general(
            tok[:, columns], mi[...], (((0,), (0,)), ((), ())), preferred_element_type=F32
        ).astype(BF16)
        start = 0
        for part in PARTS:
            cols = part_sum[:, start : start + COLS[part]]
            sums[part][zi] = cols.reshape(4, 4, 2, ROWS, COLS[part])
            start += COLS[part]

    def weight_block(zi):
        return jnp.concatenate(
            [gathered[part][zi].reshape(1024, COLS[part]) for part in PARTS], axis=1
        )

    def project(zi):
        columns = pl.ds(zi * 1024, 1024)
        value = jnp.dot(tok[:, columns], weight_block(zi), preferred_element_type=F32)
        if zi == 0:
            acc[...] = value
        else:
            acc[...] += value

    def project_end():
        def some(j, carry):
            rows = pl.ds(pl.multiple_of(j * 64, 64), 64)
            inverse = inv[rows, :]
            value = acc[rows, :] * inverse
            proj[rows, :] = value.astype(BF16)
            mean = jnp.sum(value * masked[rows, :].astype(F32), axis=1, keepdims=True) * (1.0 / D)
            coef[rows, :] = mean * inverse
            return carry

        lax.fori_loop(0, TOK // 64, some, 0)

    def backward(zi):
        columns = pl.ds(zi * 1024, 1024)
        value = lax.dot_general(
            masked[...], weight_block(zi), (((1,), (1,)), ((), ())), preferred_element_type=F32
        )
        value = inv[...] * (value - tok[:, columns].astype(F32) * coef[...])
        tok[:, columns] = value.astype(BF16)

    for i in range(4):
        for copy in load(i):
            copy.start()
    row = lax.broadcasted_iota(jnp.int32, (ROWS, ROWS), 0)
    column = lax.broadcasted_iota(jnp.int32, (ROWS, ROWS), 1)
    own_gain = jnp.sum(jnp.where(row == column, gain[...].astype(F32), 0.0), axis=1, keepdims=True)
    row2 = lax.broadcasted_iota(jnp.int32, (ROWS, ROWS // 2), 0)
    column2 = lax.broadcasted_iota(jnp.int32, (ROWS, ROWS // 2), 1)
    own_scale = jnp.sum(jnp.where(row2 // 2 == column2, scales[...].astype(F32), 0.0), axis=1, keepdims=True)
    weight = (codes[...].astype(F32) * own_scale).astype(BF16)
    mine[...] = weight
    scaled = (weight.astype(F32) * own_gain).astype(BF16)
    start = 0
    for part in PARTS:
        gathered[part][z, x, y, core] = scaled[:, start : start + COLS[part]]
        start += COLS[part]

    barrier = pltpu.get_barrier_semaphore()
    partners = [sibling] + [beside(axis, step) for axis in range(3) for step in STEPS]
    for partner in partners:
        pl.semaphore_signal(barrier, inc=1, device_id=partner, device_id_type=MESH)
    columns_of_mask = mask[...].astype(F32).T
    for i in range(8):
        coef[pl.ds(128 * i, 128), :] = columns_of_mask[:, i : i + 1]
    pl.semaphore_wait(barrier, len(partners))

    ag_send_out(0)
    norms(0)
    norms(1)
    ag_wait(0)
    ag_send_out(1)
    chunk_out(0)
    norms(2)
    norms(3)
    partial_sums(0)
    pair_out(0)
    chunk_pass(0)
    partial_sums(1)
    pair_out(1)
    ag_wait(1)
    for chunk in (1, 2, 3):
        chunk_out(chunk)
    for part in PARTS:
        forward(part, 0, 0, False).start()
    pair_add(0)
    partial_sums(2)
    pair_out(2)
    pair_add(1)
    partial_sums(3)
    pair_out(3)
    pair_add(2)
    chunk_pass(1)
    pair_add(3)
    chunk_pass(2)
    chunk_pass(3)
    for i in range(4):
        rs_begin(i)
    for chunk in range(4):
        chunk_end(chunk)
    for slot in range(4):
        forward_wait(slot)
    project(0)
    rs_pass_z(0)
    rs_pass_z(1)
    rs_pass(0)
    rs_pass(1)
    project(1)
    rs_pass(2)
    rs_pass(3)
    project(2)
    project(3)
    project_end()
    rs_own_z()
    rs_send_out(0, 1)
    for part in (1, 2):
        rs_own(part)
        rs_send_out(part, 1)
    backward(0)
    backward(1)
    backward(2)
    for part in PARTS:
        rs_total(part, 1)
        rs_send_out(part, 2)
    backward(3)
    total = jnp.concatenate([rs_total(part, 2) for part in PARTS], axis=1)
    grad_weight[...] = total * own_gain
    sums_of_rows = jnp.sum(total * mine[...].astype(F32), axis=1, keepdims=True)
    grad_gain[...] = jnp.sum(jnp.where(row == column, sums_of_rows, 0.0), axis=0, keepdims=True)

    for part in PARTS:
        for stage in (0, 1):
            for slot in range(3):
                ag_copy(part, stage, slot, False).wait_send()
                rs_copy(part, stage + 1, slot).wait_send()
        forward(part, 0, 0, False).wait_send()
        for i in range(4):
            for slot in range(4):
                ag_chunk(part, i, slot, False).wait_send()
            for slot in (1, 2, 3):
                forward(part, i, slot, False).wait_send()
            pair_copy(part, i).wait_send()
    for slot in range(6):
        z_copy(slot).wait_send()
    for part in (1, 2):
        for i in range(4):
            for kind in range(3):
                block_copy(part, i, kind).wait_send()


def store(proj, tok, grad_weight, grad_gain, *refs):
    outs, sems = refs[:4], refs[4]
    copies = [
        pltpu.make_async_copy(src, dst, sems.at[i])
        for i, (src, dst) in enumerate(zip((proj, tok, grad_weight, grad_gain), outs))
    ]
    for copy in copies:
        copy.start()
    for copy in copies:
        copy.wait()


def shards(tokens, norm_gain, weight_codes, block_scales, upstream, loss_mask):
    anywhere = pl.BlockSpec(memory_space=pl.ANY)
    vmem = pl.BlockSpec(memory_space=pltpu.VMEM)
    blocks = [pltpu.VMEM((4, 4, 4, 2, ROWS, cols), BF16) for cols in COLS]
    pairs = [pltpu.VMEM((4, 4, 4, ROWS, cols), BF16) for cols in COLS]
    landing = [
        pltpu.VMEM((6, 2, 4, ROWS, COLS[0]), BF16),
        pltpu.VMEM((12, 4, ROWS, COLS[1]), BF16),
        pltpu.VMEM((12, 4, ROWS, COLS[2]), BF16),
        *[pltpu.VMEM((3, 4, ROWS, cols), BF16) for cols in COLS],
        *[pltpu.VMEM((3, ROWS, cols), BF16) for cols in COLS],
    ]
    dma = pltpu.SemaphoreType.DMA
    shapes = (((TOK, KV), BF16), ((TOK, D), BF16), ((ROWS, KV), F32), ((1, ROWS), F32))
    results = pl.pallas_call(
        kernel,
        out_shape=tuple(pltpu.VMEM(*shape) for shape in shapes),
        in_specs=[anywhere, anywhere, vmem, vmem, vmem, vmem],
        out_specs=(vmem, vmem, vmem, vmem),
        scratch_shapes=[
            pltpu.VMEM((TOK, KV), BF16),
            pltpu.VMEM((TOK, KV), BF16),
            pltpu.VMEM((TOK, KV), BF16),
            pltpu.VMEM((TOK, 1), F32),
            pltpu.VMEM((TOK, 1), F32),
            pltpu.VMEM((TOK, KV), F32),
            pltpu.VMEM((ROWS, KV), BF16),
            *blocks,
            *blocks,
            *pairs,
            *landing,
            dma((8,)),
            dma((66,)),
            dma((66,)),
            dma((39,)),
            dma((39,)),
            dma((12,)),
            dma((12,)),
            dma((54,)),
            dma((54,)),
        ],
        compiler_params=pltpu.CompilerParams(
            collective_id=0, has_side_effects=True, vmem_limit_bytes=48 * 1024 * 1024
        ),
        name="fused_key_projection",
    )(
        tokens,
        upstream,
        loss_mask.reshape(8, 128),
        weight_codes,
        block_scales.reshape(1, ROWS // 2),
        norm_gain.reshape(1, ROWS),
    )
    projected, grad_tokens, grad_weight, grad_gain = pl.pallas_call(
        store,
        out_shape=tuple(jax.ShapeDtypeStruct(*shape) for shape in shapes),
        in_specs=[vmem] * 4,
        out_specs=(anywhere,) * 4,
        scratch_shapes=[dma((4,))],
        compiler_params=pltpu.CompilerParams(vmem_limit_bytes=1024 * 1024),
        name="store_results",
    )(*[pltpu.with_memory_space_constraint(result, pltpu.VMEM) for result in results])
    return projected, grad_tokens, grad_weight, grad_gain.reshape(ROWS)


def solution(mesh):
    both = ("intra", "cross")
    return jax.shard_map(
        shards,
        mesh=mesh,
        in_specs=(P(both, None), P(both), P(both, None), P(both), P(both, None), P(both)),
        out_specs=(P(both, None), P(both, None), P(both, None), P(both)),
        check_vma=False,
    )
```

time: 771 us -> 70.5 us (0.09)
  waiting for transfers between devices: 548 us -> 0 us
  blocking collectives: 134 us -> 0 us
  Pallas kernels: 0 us -> 69.5 us
  matrix products: 45.1 us -> 0 us
  other arithmetic: 18.9 us -> 0 us
  between operations: 14.1 us -> 0.82 us
    reduce_scatter x1 -> x0, waiting for transfers between devices: 547 us -> none  [shards(): lax.psum_scatter(part_weight, ('intra', 'cross'), scatter_dimension=0, ti...]
    unnamed x2 -> x0, blocking collectives: 134 us -> none
    pallas_call x0 -> x2, Pallas kernels: none -> 69.5 us  [the longest x1 65.4 us: shards(): pl.pallas_call(kernel, out_shape=tuple((pltpu.VMEM(*shape) for shape in s...]
    dot_general x3 -> x0, matrix products: 45.1 us -> none  [the longest x1 16.6 us: shards(): lax.dot_general(masked, weight_rows, (((1,), (1,)), ((), ())), preferred_...]
    convert_element_type x4 -> x0, other arithmetic: 13.7 us -> none  [the longest x1 13 us: shards(): grad_tokens = (inverse * (grad_scaled - unit_rows * jnp.mean(grad_scaled...]
  transfers between devices with their start and end apart: 2 -> 0, of which waited for: 1 -> 0; matrix products, arithmetic and copies ran while one was open for 9% -> 0% of each run, Pallas kernels for 0% -> 0%
where the time goes in v1:
time: 70.5 us; the launch traced here: 70.3 us
  Pallas kernels  69.5 us (99%)
  between operations  0.82 us (1%)
    pallas_call x1, Pallas kernels, shards(): pl.pallas_call(kernel, out_shape=tuple((pltpu.VMEM(*shape) for shape in s...  65.4 us
    pallas_call x1, Pallas kernels, shards(): pl.pallas_call(store, out_shape=tuple((jax.ShapeDtypeStruct(*shape) for s...  4.14 us

profile of v1, /device:TPU:1, one launch (start us, length us, event | category | flops | bytes accessed | tf_op | source)
XLA Modules:
  0.0 70.3 jit_solution(16900712484190870779)
XLA Ops:
  0.6 65.4 %fused_key_projection.1 = (bf16[1024,1024]{1,0:T(8,128)(2,1)S(1)}, bf16[1024,4096]{1,0:T(8,128)(2,1)S(1)}, f32[32,1024]{1,0:T(8,128)S(1)}, f32[1,32]{1,0:T(1,128)S(1)}) custom-call(bf16[1024,4096]{1,0:T(8,128)(2,1)} %tokens.1, bf16[1024,1024]{1,0:T(8,128)(2,1)} %upstream.1, s32[8,128]{1,0:T(8,128)} %bitcast.4, bf16[32,1024]{1,0:T(8,128)(2,1)} %codes.1, ...), custom_call_target="tpu_custom_call" | custom-call | tf_op jit(solution)/shard_map/fused_key_projection/pallas_call | solution.py:446
  66.0 4.1 %store_results.1 = (bf16[1024,1024]{1,0:T(8,128)(2,1)}, bf16[1024,4096]{1,0:T(8,128)(2,1)}, f32[32,1024]{1,0:T(8,128)}, f32[1,32]{1,0:T(1,128)}) custom-call(bf16[1024,1024]{1,0:T(8,128)(2,1)S(1)} %get-tuple-element.12.proj, bf16[1024,4096]{1,0:T(8,128)(2,1)S(1)} %get-tuple-element.13.tok, f32[32,1024]{1,0:T(8,128)S(1)} %get-tuple-element.14.grad_weight, ...), custom_call_target="tpu_custom_call" | custom-call | tf_op jit(solution)/shard_map/store_results/pallas_call | solution.py:485

commit v2 on v1

--- a/solution.py
+++ b/solution.py
@@ -177,11 +177,17 @@
         step = (2, 1, -1)[kind]
         return rs_remote(part, 0, kind * 4 + i, block_index(part, i, shifted(axis, step)), axis, side)
 
-    def rs_begin(i):
-        for slot in ((0, 1), (3,), (4,), ())[i]:
-            z_copy(slot).start()
+    def rs_across(i):
+        if i == 0:
+            z_copy(0).start()
+            z_copy(1).start()
         for part in (1, 2):
             block_copy(part, i, 0).start()
+
+    def rs_direct(i):
+        if i in (1, 2):
+            z_copy(2 + i).start()
+        for part in (1, 2):
             block_copy(part, i, 2 if i < 2 else 1).start()
 
     def rs_pass_z(slot):
@@ -280,25 +286,38 @@
             [gathered[part][zi].reshape(1024, COLS[part]) for part in PARTS], axis=1
         )
 
-    def project(zi):
-        columns = pl.ds(zi * 1024, 1024)
-        value = jnp.dot(tok[:, columns], weight_block(zi), preferred_element_type=F32)
-        if zi == 0:
-            acc[...] = value
+    def project(part, number, at):
+        start = sum(COLS[:part])
+        cols = slice(start, start + COLS[part])
+        if part == 0:
+            left, right = tok[:, pl.ds(pl.multiple_of(at * 1024, 1024), 1024)], gathered[0][at].reshape(1024, COLS[0])
+        elif part == 1:
+            left = [tok[:, pl.ds(pl.multiple_of(zi * 1024 + at * 256, 256), 256)] for zi in range(4)]
+            right = [gathered[1][zi, at].reshape(256, COLS[1]) for zi in range(4)]
+            left, right = jnp.concatenate(left, axis=1), jnp.concatenate(right, axis=0)
         else:
-            acc[...] += value
+            left, right = tok[...], gathered[2][...].reshape(D, COLS[2])
+        value = jnp.dot(left, right, preferred_element_type=F32)
+        if number == 0:
+            acc[:, cols] = value
+        else:
+            acc[:, cols] += value
+
+    def project_planes(slot):
+        for part in (0, 1):
+            project(part, slot, shifted(ORDERS[part][0], PLANES[slot]))
 
     def project_end():
-        def some(j, carry):
-            rows = pl.ds(pl.multiple_of(j * 64, 64), 64)
+        def some(j):
+            rows = pl.ds(j * 64, 64)
             inverse = inv[rows, :]
             value = acc[rows, :] * inverse
             proj[rows, :] = value.astype(BF16)
             mean = jnp.sum(value * masked[rows, :].astype(F32), axis=1, keepdims=True) * (1.0 / D)
             coef[rows, :] = mean * inverse
-            return carry
-
-        lax.fori_loop(0, TOK // 64, some, 0)
+
+        for j in range(TOK // 64):
+            some(j)
 
     def backward(zi):
         columns = pl.ds(zi * 1024, 1024)
@@ -308,6 +327,10 @@
         value = inv[...] * (value - tok[:, columns].astype(F32) * coef[...])
         tok[:, columns] = value.astype(BF16)
 
+    barrier = pltpu.get_barrier_semaphore()
+    partners = [sibling] + [beside(axis, step) for axis in range(3) for step in STEPS]
+    for partner in partners:
+        pl.semaphore_signal(barrier, inc=1, device_id=partner, device_id_type=MESH)
     for i in range(4):
         for copy in load(i):
             copy.start()
@@ -325,10 +348,6 @@
         gathered[part][z, x, y, core] = scaled[:, start : start + COLS[part]]
         start += COLS[part]
 
-    barrier = pltpu.get_barrier_semaphore()
-    partners = [sibling] + [beside(axis, step) for axis in range(3) for step in STEPS]
-    for partner in partners:
-        pl.semaphore_signal(barrier, inc=1, device_id=partner, device_id_type=MESH)
     columns_of_mask = mask[...].astype(F32).T
     for i in range(8):
         coef[pl.ds(128 * i, 128), :] = columns_of_mask[:, i : i + 1]
@@ -344,7 +363,6 @@
     norms(3)
     partial_sums(0)
     pair_out(0)
-    chunk_pass(0)
     partial_sums(1)
     pair_out(1)
     ag_wait(1)
@@ -355,37 +373,43 @@
     pair_add(0)
     partial_sums(2)
     pair_out(2)
+    chunk_pass(0)
     pair_add(1)
+    rs_across(0)
+    rs_across(1)
     partial_sums(3)
     pair_out(3)
     pair_add(2)
+    rs_across(2)
     chunk_pass(1)
     pair_add(3)
+    rs_across(3)
     chunk_pass(2)
     chunk_pass(3)
     for i in range(4):
-        rs_begin(i)
+        rs_direct(i)
+    forward_wait(0)
+    project_planes(0)
+    forward_wait(1)
+    project_planes(1)
+    rs_pass_z(0)
+    rs_pass_z(1)
+    for i in range(4):
+        rs_pass(i)
+    forward_wait(2)
+    project_planes(2)
     for chunk in range(4):
         chunk_end(chunk)
-    for slot in range(4):
-        forward_wait(slot)
-    project(0)
-    rs_pass_z(0)
-    rs_pass_z(1)
-    rs_pass(0)
-    rs_pass(1)
-    project(1)
-    rs_pass(2)
-    rs_pass(3)
-    project(2)
-    project(3)
+    forward_wait(3)
+    project_planes(3)
+    project(2, 0, 0)
     project_end()
+    backward(0)
     rs_own_z()
     rs_send_out(0, 1)
     for part in (1, 2):
         rs_own(part)
         rs_send_out(part, 1)
-    backward(0)
     backward(1)
     backward(2)
     for part in PARTS:

time: 70.5 us -> 65.4 us (0.928)
  Pallas kernels: 69.5 us -> 64.4 us
    pallas_call x1, Pallas kernels: 65.4 us -> 60.3 us  [shards(): pl.pallas_call(kernel, out_shape=tuple((pltpu.VMEM(*shape) for shape in s...]
where the time goes in v2:
time: 65.4 us; the launch traced here: 65.2 us
  Pallas kernels  64.4 us (98%)
  between operations  0.82 us (1%)
    pallas_call x1, Pallas kernels, shards(): pl.pallas_call(kernel, out_shape=tuple((pltpu.VMEM(*shape) for shape in s...  60.3 us
    pallas_call x1, Pallas kernels, shards(): pl.pallas_call(store, out_shape=tuple((jax.ShapeDtypeStruct(*shape) for s...  4.14 us

profile of v2, /device:TPU:1, one launch (start us, length us, event | category | flops | bytes accessed | tf_op | source)
XLA Modules:
  0.0 65.2 jit_solution(1408226741803701600)
XLA Ops:
  0.6 60.3 %fused_key_projection.1 = (bf16[1024,1024]{1,0:T(8,128)(2,1)S(1)}, bf16[1024,4096]{1,0:T(8,128)(2,1)S(1)}, f32[32,1024]{1,0:T(8,128)S(1)}, f32[1,32]{1,0:T(1,128)S(1)}) custom-call(bf16[1024,4096]{1,0:T(8,128)(2,1)} %tokens.1, bf16[1024,1024]{1,0:T(8,128)(2,1)} %upstream.1, s32[8,128]{1,0:T(8,128)} %bitcast.4, bf16[32,1024]{1,0:T(8,128)(2,1)} %codes.1, ...), custom_call_target="tpu_custom_call" | custom-call | tf_op jit(solution)/shard_map/fused_key_projection/pallas_call | solution.py:470
  60.9 4.1 %store_results.1 = (bf16[1024,1024]{1,0:T(8,128)(2,1)}, bf16[1024,4096]{1,0:T(8,128)(2,1)}, f32[32,1024]{1,0:T(8,128)}, f32[1,32]{1,0:T(1,128)}) custom-call(bf16[1024,1024]{1,0:T(8,128)(2,1)S(1)} %get-tuple-element.12.proj, bf16[1024,4096]{1,0:T(8,128)(2,1)S(1)} %get-tuple-element.13.tok, f32[32,1024]{1,0:T(8,128)S(1)} %get-tuple-element.14.grad_weight, ...), custom_call_target="tpu_custom_call" | custom-call | tf_op jit(solution)/shard_map/store_results/pallas_call | solution.py:509

commit v3 on v2

--- a/solution.py
+++ b/solution.py
@@ -386,8 +386,6 @@
     rs_across(3)
     chunk_pass(2)
     chunk_pass(3)
-    for i in range(4):
-        rs_direct(i)
     forward_wait(0)
     project_planes(0)
     forward_wait(1)
@@ -396,10 +394,12 @@
     rs_pass_z(1)
     for i in range(4):
         rs_pass(i)
+    for i in range(4):
+        rs_direct(i)
+    for chunk in range(4):
+        chunk_end(chunk)
     forward_wait(2)
     project_planes(2)
-    for chunk in range(4):
-        chunk_end(chunk)
     forward_wait(3)
     project_planes(3)
     project(2, 0, 0)

time: 65.4 us -> 63.8 us (0.976)
  Pallas kernels: 64.4 us -> 62.8 us
    pallas_call x1, Pallas kernels: 60.3 us -> 58.7 us  [shards(): pl.pallas_call(kernel, out_shape=tuple((pltpu.VMEM(*shape) for shape in s...]
where the time goes in v3:
time: 63.8 us; the launch traced here: 63.6 us
  Pallas kernels  62.8 us (98%)
  between operations  0.82 us (1%)
    pallas_call x1, Pallas kernels, shards(): pl.pallas_call(kernel, out_shape=tuple((pltpu.VMEM(*shape) for shape in s...  58.7 us
    pallas_call x1, Pallas kernels, shards(): pl.pallas_call(store, out_shape=tuple((jax.ShapeDtypeStruct(*shape) for s...  4.14 us

profile of v3, /device:TPU:1, one launch (start us, length us, event | category | flops | bytes accessed | tf_op | source)
XLA Modules:
  0.0 63.6 jit_solution(18424645935704180816)
XLA Ops:
  0.6 58.7 %fused_key_projection.1 = (bf16[1024,1024]{1,0:T(8,128)(2,1)S(1)}, bf16[1024,4096]{1,0:T(8,128)(2,1)S(1)}, f32[32,1024]{1,0:T(8,128)S(1)}, f32[1,32]{1,0:T(1,128)S(1)}) custom-call(bf16[1024,4096]{1,0:T(8,128)(2,1)} %tokens.1, bf16[1024,1024]{1,0:T(8,128)(2,1)} %upstream.1, s32[8,128]{1,0:T(8,128)} %bitcast.4, bf16[32,1024]{1,0:T(8,128)(2,1)} %codes.1, ...), custom_call_target="tpu_custom_call" | custom-call | tf_op jit(solution)/shard_map/fused_key_projection/pallas_call | solution.py:470
  59.3 4.1 %store_results.1 = (bf16[1024,1024]{1,0:T(8,128)(2,1)}, bf16[1024,4096]{1,0:T(8,128)(2,1)}, f32[32,1024]{1,0:T(8,128)}, f32[1,32]{1,0:T(1,128)}) custom-call(bf16[1024,1024]{1,0:T(8,128)(2,1)S(1)} %get-tuple-element.12.proj, bf16[1024,4096]{1,0:T(8,128)(2,1)S(1)} %get-tuple-element.13.tok, f32[32,1024]{1,0:T(8,128)S(1)} %get-tuple-element.14.grad_weight, ...), custom_call_target="tpu_custom_call" | custom-call | tf_op jit(solution)/shard_map/store_results/pallas_call | solution.py:509
